TPU v7x, 32 devices: a whole 2x2x4 slice. The times are simulated.
32 devices in a mesh: fsdp: 2 (over x), context: 16 (over z, y, core).
Axes of the slice: x: 2, y: 2, z: 4, core: 2. Of those that a mesh axis runs over, the one named last changes fastest.
Arguments:
- tokens: bfloat16 [2, 2048, 1600], P('fsdp', 'context'), may hold values from -6 to 6
- cotangent: bfloat16 [2, 2048, 1600], P('fsdp', 'context'), may hold values from -6 to 6
- block_order: int32 [32], replicated, may hold values from 0 to 31, each once
- ln1_gain: bfloat16 [1600], P('fsdp'), may hold values from 0.5 to 1.5
- ln1_bias: bfloat16 [1600], P('fsdp'), may hold values from -3 to 3
- w_qkv: bfloat16 [1600, 4800], P('context', 'fsdp'), may hold values from -5.05 to 5.05
- qv_bias: bfloat16 [1600, 2], P('fsdp'), may hold values from -0.29882812 to 0.29882812
- w_out: bfloat16 [1600, 1600], P('context', 'fsdp'), may hold values from -0.875 to 0.875
- out_bias: bfloat16 [1600], P('fsdp'), may hold values from -3 to 3
- ln2_gain: bfloat16 [1600], P('fsdp'), may hold values from 0.5 to 1.5
- ln2_bias: bfloat16 [1600], P('fsdp'), may hold values from -3 to 3
- w_fc: bfloat16 [1600, 6400], P('context', 'fsdp'), may hold values from -0.15625 to 0.15625
- fc_bias: bfloat16 [6400], P('fsdp'), may hold values from -3 to 3
- w_proj: bfloat16 [6400, 1600], P('context', 'fsdp'), may hold values from -0.078125 to 0.078125
- proj_bias: bfloat16 [1600], P('fsdp'), may hold values from -3 to 3
Outputs:
- out: bfloat16 [2, 2048, 1600], P('fsdp', 'context')
- d_tokens: bfloat16 [2, 2048, 1600], P('fsdp', 'context')
- g_ln1_gain: float32 [1600], P('fsdp')
- g_ln1_bias: float32 [1600], P('fsdp')
- g_w_qkv: float32 [1600, 4800], P('context', 'fsdp')
- g_qv_bias: float32 [1600, 2], P('fsdp')
- g_w_out: float32 [1600, 1600], P('context', 'fsdp')
- g_out_bias: float32 [1600], P('fsdp')
- g_ln2_gain: float32 [1600], P('fsdp')
- g_ln2_bias: float32 [1600], P('fsdp')
- g_w_fc: float32 [1600, 6400], P('context', 'fsdp')
- g_fc_bias: float32 [6400], P('fsdp')
- g_w_proj: float32 [6400, 1600], P('context', 'fsdp')
- g_proj_bias: float32 [1600], P('fsdp')
Inputs may be any that keep to these rules, and one draw needn't show every extreme that they name: block_order names each of the 32 blocks of positions once; rows s * 64 to s * 64 + 63 of a sequence hold positions block_order[s] * 64 onward, in order.
All inputs are finite; a program needn't handle non-finite values.
Results may differ from a plain program's by a relative error of at most 0.025.
Values may be sent and summed in bfloat16 or wider, within the bound.
No kernel may reach another device: no remote copies, remote signals or barrier semaphores. Data moves between devices by JAX's collectives and lax.ppermute only.
A program may use at most 576 MiB of HBM per device.

v0:
```python
import math
import jax
import jax.numpy as jnp
from jax import lax
from jax.sharding import PartitionSpec as P

HEADS = 25
HEAD_DIM = 64
EPSILON = 1e-05
GELU_ROOT = math.sqrt(2.0 / math.pi)
GELU_CUBIC = 0.044715
NEG_LARGE = -1e30


def normalize(values, gain_vec, bias_vec):
    centred = values - jnp.mean(values, axis=-1, keepdims=True)
    inv_std = lax.rsqrt(jnp.mean(centred * centred, axis=-1, keepdims=True) + EPSILON)
    normed = centred * inv_std
    return (normed * gain_vec.astype(jnp.float32) + bias_vec.astype(jnp.float32), normed, inv_std)


def norm_back(upstream, normed, inv_std, gain_vec):
    scaled = upstream * gain_vec.astype(jnp.float32)
    return inv_std * (
        scaled
        - jnp.mean(scaled, axis=-1, keepdims=True)
        - normed * jnp.mean(scaled * normed, axis=-1, keepdims=True)
    )


def gelu_pair(pre_act):
    inner = GELU_ROOT * (pre_act + GELU_CUBIC * pre_act * pre_act * pre_act)
    tangent = jnp.tanh(inner)
    act_value = 0.5 * pre_act * (1.0 + tangent)
    act_slope = 0.5 * (1.0 + tangent) + 0.5 * pre_act * (1.0 - tangent * tangent) * GELU_ROOT * (
        1.0 + 3.0 * GELU_CUBIC * pre_act * pre_act
    )
    return (act_value, act_slope)


def positions_of(block_order, block_len):
    offsets = jnp.arange(block_len, dtype=jnp.int32)
    return (block_order[:, None] * block_len + offsets[None, :]).reshape(-1)


def gather_rows(first, second):
    return (
        lax.all_gather(first, "context", axis=0, tiled=True),
        lax.all_gather(second, "context", axis=0, tiled=True),
    )


def gather_cols(first, second, vec_a, vec_b, vec_c, vec_d):
    return (
        lax.all_gather(first, "fsdp", axis=1, tiled=True),
        lax.all_gather(second, "fsdp", axis=1, tiled=True),
        lax.all_gather(vec_a, "fsdp", axis=0, tiled=True),
        lax.all_gather(vec_b, "fsdp", axis=0, tiled=True),
        lax.all_gather(vec_c, "fsdp", axis=0, tiled=True),
        lax.all_gather(vec_d, "fsdp", axis=0, tiled=True),
    )


def fetch(first, second, vec_a, vec_b, vec_c, vec_d):
    cols = gather_cols(first, second, vec_a, vec_b, vec_c, vec_d)
    rows = gather_rows(cols[0], cols[1])
    return (rows[0], rows[1], cols[2], cols[3], cols[4], cols[5])


def scatter_rows(first, second):
    return (
        lax.psum_scatter(first, "context", scatter_dimension=0, tiled=True),
        lax.psum_scatter(second, "context", scatter_dimension=0, tiled=True),
    )


def scatter_cols(first, second, vec_a, vec_b, vec_c, vec_d):
    return (
        lax.psum_scatter(
            first.astype(jnp.bfloat16), "fsdp", scatter_dimension=1, tiled=True
        ).astype(jnp.float32),
        lax.psum_scatter(
            second.astype(jnp.bfloat16), "fsdp", scatter_dimension=1, tiled=True
        ).astype(jnp.float32),
        lax.psum_scatter(
            vec_a.astype(jnp.bfloat16), "fsdp", scatter_dimension=0, tiled=True
        ).astype(jnp.float32),
        lax.psum_scatter(
            vec_b.astype(jnp.bfloat16), "fsdp", scatter_dimension=0, tiled=True
        ).astype(jnp.float32),
        lax.psum_scatter(
            vec_c.astype(jnp.bfloat16), "fsdp", scatter_dimension=0, tiled=True
        ).astype(jnp.float32),
        lax.psum_scatter(
            vec_d.astype(jnp.bfloat16), "fsdp", scatter_dimension=0, tiled=True
        ).astype(jnp.float32),
    )


def send_grads(first, second, vec_a, vec_b, vec_c, vec_d):
    rows = scatter_rows(first, second)
    return scatter_cols(rows[0], rows[1], vec_a, vec_b, vec_c, vec_d)


def attend_forward(query_heads, keys_all, values_all, query_pos, key_pos):
    length = keys_all.shape[0]
    rows_here = query_heads.shape[0]
    kblock = math.gcd(length, 512)
    nblocks = length // kblock
    score_scale = HEAD_DIM ** (-0.5)
    key_blocks = keys_all.reshape(nblocks, kblock, HEADS, HEAD_DIM)
    value_blocks = values_all.reshape(nblocks, kblock, HEADS, HEAD_DIM)
    pos_blocks = key_pos.reshape(nblocks, kblock)

    def step(carry, inputs):
        maxima, totals, accum = carry
        block_keys, block_values, block_pos = inputs
        scores = (
            jnp.einsum("qhd,khd->hqk", query_heads, block_keys, preferred_element_type=jnp.float32)
            * score_scale
        )
        allowed = (query_pos[:, None] >= block_pos[None, :])[None]
        fresh = jnp.maximum(maxima, jnp.max(jnp.where(allowed, scores, NEG_LARGE), axis=-1))
        exp_terms = jnp.where(allowed, jnp.exp(scores - fresh[..., None]), 0.0)
        decay_factor = jnp.exp(maxima - fresh)
        totals = totals * decay_factor + jnp.sum(exp_terms, axis=-1)
        accum = accum * decay_factor[..., None] + jnp.einsum(
            "hqk,khd->hqd",
            exp_terms.astype(jnp.bfloat16),
            block_values,
            preferred_element_type=jnp.float32,
        )
        return ((fresh, totals, accum), None)

    start_carry = (
        jnp.full((HEADS, rows_here), NEG_LARGE, jnp.float32),
        jnp.zeros((HEADS, rows_here), jnp.float32),
        jnp.zeros((HEADS, rows_here, HEAD_DIM), jnp.float32),
    )
    (maxima, totals, accum), _ = lax.scan(step, start_carry, (key_blocks, value_blocks, pos_blocks))
    attn_out = (accum / totals[..., None]).transpose(1, 0, 2).reshape(rows_here, HEADS * HEAD_DIM)
    return (attn_out.astype(jnp.bfloat16), maxima + jnp.log(totals))


def block_terms(
    query_heads, grad_heads, row_dot, log_norm, query_pos, block_keys, block_values, block_pos
):
    score_scale = HEAD_DIM ** (-0.5)
    scores = (
        jnp.einsum("qhd,khd->hqk", query_heads, block_keys, preferred_element_type=jnp.float32)
        * score_scale
    )
    allowed = (query_pos[:, None] >= block_pos[None, :])[None]
    prob_full = jnp.where(allowed, jnp.exp(scores - log_norm[..., None]), 0.0)
    prob_half = prob_full.astype(jnp.bfloat16)
    value_grad = jnp.einsum(
        "hqk,qhd->khd", prob_half, grad_heads, preferred_element_type=jnp.float32
    )
    dprob = jnp.einsum("qhd,khd->hqk", grad_heads, block_values, preferred_element_type=jnp.float32)
    dscore = (score_scale * prob_full * (dprob - row_dot[..., None])).astype(jnp.bfloat16)
    query_grad = jnp.einsum("hqk,khd->qhd", dscore, block_keys, preferred_element_type=jnp.float32)
    key_grad = jnp.einsum("hqk,qhd->khd", dscore, query_heads, preferred_element_type=jnp.float32)
    return (query_grad, key_grad, value_grad)


def attend_backward(
    query_heads, keys_all, values_all, query_pos, key_pos, log_norm, grad_o16, attn_out
):
    length = keys_all.shape[0]
    rows_here = query_heads.shape[0]
    width = HEADS * HEAD_DIM
    kblock = math.gcd(length, 512)
    nblocks = length // kblock
    grad_heads = grad_o16.reshape(rows_here, HEADS, HEAD_DIM)
    row_dot = jnp.sum(
        grad_o16.astype(jnp.float32).reshape(rows_here, HEADS, HEAD_DIM)
        * attn_out.astype(jnp.float32).reshape(rows_here, HEADS, HEAD_DIM),
        axis=-1,
    ).T
    key_blocks = keys_all.reshape(nblocks, kblock, HEADS, HEAD_DIM)
    value_blocks = values_all.reshape(nblocks, kblock, HEADS, HEAD_DIM)
    pos_blocks = key_pos.reshape(nblocks, kblock)
    start_grad = jnp.zeros((rows_here, HEADS, HEAD_DIM), jnp.float32)

    def step_whole(carry, inputs):
        query_grad, key_grad, value_grad = block_terms(
            query_heads, grad_heads, row_dot, log_norm, query_pos, inputs[0], inputs[1], inputs[2]
        )
        return (carry + query_grad, (key_grad, value_grad))

    query_total, (key_parts, value_parts) = lax.scan(
        step_whole, start_grad, (key_blocks, value_blocks, pos_blocks)
    )
    term = jnp.concatenate(
        [key_parts.reshape(length, width), value_parts.reshape(length, width)], axis=1
    )
    owned = lax.psum_scatter(term, "context", scatter_dimension=0, tiled=True)
    key_owned, value_owned = (owned[:, :width], owned[:, width:])
    return (query_total.reshape(rows_here, width), key_owned, value_owned)


def body(
    tokens,
    cotangent,
    block_order,
    ln1_gain,
    ln1_bias,
    w_qkv,
    qv_bias,
    w_out,
    out_bias,
    ln2_gain,
    ln2_bias,
    w_fc,
    fc_bias,
    w_proj,
    proj_bias,
):
    width = HEADS * HEAD_DIM
    rows_here = tokens.shape[1]
    block_len = rows_here // 2
    grad_scale = 1.0 / math.sqrt(lax.axis_size("fsdp") * lax.axis_size("context") * rows_here)
    key_pos = positions_of(block_order, block_len)
    query_pos = lax.dynamic_slice_in_dim(key_pos, lax.axis_index("context") * rows_here, rows_here)
    w_qkv_all, w_out_all, gain_one, shift_one, qv_all, out_b = fetch(
        w_qkv, w_out, ln1_gain, ln1_bias, qv_bias, out_bias
    )
    w_fc_all, w_proj_all, gain_two, shift_two, fc_b, proj_b = fetch(
        w_fc, w_proj, ln2_gain, ln2_bias, fc_bias, proj_bias
    )
    xs = tokens[0].astype(jnp.float32)
    h_one, normed_one, inv_one = normalize(xs, gain_one, shift_one)
    h_one = h_one.astype(jnp.bfloat16)
    qkv = jnp.dot(h_one, w_qkv_all, preferred_element_type=jnp.float32)
    queries = (qkv[:, :width] + qv_all[:, 0].astype(jnp.float32)).astype(jnp.bfloat16)
    key_rows = qkv[:, width : 2 * width].astype(jnp.bfloat16)
    value_rows = (qkv[:, 2 * width :] + qv_all[:, 1].astype(jnp.float32)).astype(jnp.bfloat16)
    keys_all, values_all = (
        lax.all_gather(key_rows, "context", axis=0, tiled=True),
        lax.all_gather(value_rows, "context", axis=0, tiled=True),
    )
    query_heads = queries.reshape(rows_here, HEADS, HEAD_DIM)
    attn_out, log_norm = attend_forward(query_heads, keys_all, values_all, query_pos, key_pos)
    resid_one = (
        xs
        + jnp.dot(attn_out, w_out_all, preferred_element_type=jnp.float32)
        + out_b.astype(jnp.float32)
    )
    h_two, normed_two, inv_two = normalize(resid_one, gain_two, shift_two)
    h_two = h_two.astype(jnp.bfloat16)
    pre_act = jnp.dot(h_two, w_fc_all, preferred_element_type=jnp.float32) + fc_b.astype(
        jnp.float32
    )
    act_value, act_slope = gelu_pair(pre_act)
    act_half = act_value.astype(jnp.bfloat16)
    result = (
        resid_one
        + jnp.dot(act_half, w_proj_all, preferred_element_type=jnp.float32)
        + proj_b.astype(jnp.float32)
    )
    cot_rows = cotangent[0]
    grad_y = cot_rows.astype(jnp.float32)
    g_w_proj = jnp.dot(act_half.T, cot_rows, preferred_element_type=jnp.float32) * grad_scale
    g_proj_bias = jnp.sum(grad_y, axis=0) * grad_scale
    grad_pre = jnp.dot(cot_rows, w_proj_all.T, preferred_element_type=jnp.float32) * act_slope
    g_fc_bias = jnp.sum(grad_pre, axis=0) * grad_scale
    grad_pre16 = grad_pre.astype(jnp.bfloat16)
    g_w_fc = jnp.dot(h_two.T, grad_pre16, preferred_element_type=jnp.float32) * grad_scale
    grad_h2 = jnp.dot(grad_pre16, w_fc_all.T, preferred_element_type=jnp.float32)
    g_ln2_gain = jnp.sum(grad_h2 * normed_two, axis=0) * grad_scale
    g_ln2_bias = jnp.sum(grad_h2, axis=0) * grad_scale
    mlp_grads = send_grads(g_w_fc, g_w_proj, g_ln2_gain, g_ln2_bias, g_fc_bias, g_proj_bias)
    grad_r1 = grad_y + norm_back(grad_h2, normed_two, inv_two, gain_two)
    g_out_bias = jnp.sum(grad_r1, axis=0) * grad_scale
    grad_r16 = grad_r1.astype(jnp.bfloat16)
    g_w_out = jnp.dot(attn_out.T, grad_r16, preferred_element_type=jnp.float32) * grad_scale
    grad_o16 = jnp.dot(grad_r16, w_out_all.T, preferred_element_type=jnp.float32).astype(
        jnp.bfloat16
    )
    grad_q, grad_k, grad_v = attend_backward(
        query_heads, keys_all, values_all, query_pos, key_pos, log_norm, grad_o16, attn_out
    )
    g_qv_bias = jnp.stack([jnp.sum(grad_q, axis=0), jnp.sum(grad_v, axis=0)], axis=1) * grad_scale
    grad_qkv16 = jnp.concatenate([grad_q, grad_k, grad_v], axis=1).astype(jnp.bfloat16)
    g_w_qkv = jnp.dot(h_one.T, grad_qkv16, preferred_element_type=jnp.float32) * grad_scale
    grad_h1 = jnp.dot(grad_qkv16, w_qkv_all.T, preferred_element_type=jnp.float32)
    g_ln1_gain = jnp.sum(grad_h1 * normed_one, axis=0) * grad_scale
    g_ln1_bias = jnp.sum(grad_h1, axis=0) * grad_scale
    grad_x = (grad_r1 + norm_back(grad_h1, normed_one, inv_one, gain_one)).astype(jnp.bfloat16)
    attn_grads = send_grads(g_w_qkv, g_w_out, g_ln1_gain, g_ln1_bias, g_qv_bias, g_out_bias)
    summed = lax.psum(
        (
            attn_grads[2],
            attn_grads[3],
            attn_grads[4],
            attn_grads[5],
            mlp_grads[2],
            mlp_grads[3],
            mlp_grads[4],
            mlp_grads[5],
        ),
        "context",
    )
    return (
        result.astype(jnp.bfloat16)[None],
        grad_x[None],
        summed[0],
        summed[1],
        attn_grads[0],
        summed[2],
        attn_grads[1],
        summed[3],
        summed[4],
        summed[5],
        mlp_grads[0],
        summed[6],
        mlp_grads[1],
        summed[7],
    )


def solution(mesh):
    placed = (
        P("fsdp", "context", None),
        P("fsdp", "context", None),
        P(),
        P("fsdp"),
        P("fsdp"),
        P("context", "fsdp"),
        P("fsdp", None),
        P("context", "fsdp"),
        P("fsdp"),
        P("fsdp"),
        P("fsdp"),
        P("context", "fsdp"),
        P("fsdp"),
        P("context", "fsdp"),
        P("fsdp"),
    )
    return jax.shard_map(
        body,
        mesh=mesh,
        in_specs=placed,
        out_specs=(
            P("fsdp", "context", None),
            P("fsdp", "context", None),
            P("fsdp"),
            P("fsdp"),
            P("context", "fsdp"),
            P("fsdp", None),
            P("context", "fsdp"),
            P("fsdp"),
            P("fsdp"),
            P("fsdp"),
            P("context", "fsdp"),
            P("fsdp"),
            P("context", "fsdp"),
            P("fsdp"),
        ),
        check_vma=False,
    )
```

profile of v0, /device:TPU:0, one launch (start us, length us, event | category | flops | bytes accessed | tf_op | source)
XLA Modules:
  0.0 2697.7 jit_solution(1883228032706122756)
XLA Ops:
  8.0 18.5 all-gather
  29.9 11.2 all-gather.3
  45.6 8.7 all-reduce.21
  59.3 110.0 %all-gather.25.cloned.1.call-done = bf16[16,100,4800]{2,1,0:T(8,128)(2,1)} async-done(((bf16[1,100,4800]{2,1,0:T(8,128)(2,1)}), bf16[16,100,4800]{2,1,0:T(8,128)(2,1)}) %all-gather.25.cloned.1.call-update) | async-done | bytes 15360016 | tf_op jit(solution)/shard_map/all_gather | solution.py:48
  169.4 16.1 reshape.225
  185.5 12.2 fusion.101
  212.7 42.3 %all-gather.27.cloned.1.call-done = bf16[16,100,1600]{2,1,0:T(8,128)(2,1)} async-done(((bf16[1,100,1600]{2,1,0:T(8,128)(2,1)}), bf16[16,100,1600]{2,1,0:T(8,128)(2,1)}) %all-gather.27.cloned.1.call-update) | async-done | bytes 5120016 | tf_op jit(solution)/shard_map/all_gather | solution.py:49
  255.0 8.2 reshape.231
  263.2 102.2 %all-gather.29.cloned.1.call-done = bf16[16,100,6400]{2,1,0:T(8,128)(2,1)} async-done(((bf16[1,100,6400]{2,1,0:T(8,128)(2,1)}), bf16[16,100,6400]{2,1,0:T(8,128)(2,1)}) %all-gather.29.cloned.1.call-update) | async-done | bytes 20480016 | tf_op jit(solution)/shard_map/all_gather | solution.py:48
  365.4 17.2 reshape.233
  382.7 52.6 %all-gather.19.cloned.1.call-done = bf16[2048,1600]{0,1:T(8,128)(2,1)} async-done(((bf16[128,1600]{0,1:T(8,128)(2,1)}), bf16[2048,1600]{0,1:T(8,128)(2,1)}) %all-gather.19.cloned.1.call-update) | async-done | bytes 6553616 | tf_op jit(solution)/shard_map/all_gather | solution.py:240
  435.2 14.5 reshape.196
  449.7 7.2 copy.59
  456.9 46.5 %all-gather.17.cloned.1.call-done = bf16[2048,1600]{0,1:T(8,128)(2,1)} async-done(((bf16[128,1600]{0,1:T(8,128)(2,1)}), bf16[2048,1600]{0,1:T(8,128)(2,1)}) %all-gather.17.cloned.1.call-update) | async-done | bytes 6553616 | tf_op jit(solution)/shard_map/all_gather | solution.py:239
  503.4 14.5 reshape.194
  517.9 7.2 copy.58
  525.1 31.6 %while.30 = (s32[]{:T(128)}, f32[25,128]{1,0:T(8,128)S(1)}, f32[25,128]{1,0:T(8,128)S(1)}, f32[25,128,64]{1,2,0:T(8,128)S(1)}, s32[128]{0:T(128)S(1)}, /*index=5...) while((s32[]{:T(128)}, f32[25,128]{1,0:T(8,128)S(1)}, ...), condition=%wide.region_5.6_spmd.clone, body=%wide.region_2.5_spmd.clone.sunk | while | flops 438148736 | bytes 25459340 | solution.py:140
  562.1 12.4 convolution_add_fusion
  574.5 39.6 %all-gather.23.cloned.1.call-done = bf16[6400,1600]{1,0:T(8,128)(2,1)} async-done(((bf16[400,1600]{1,0:T(8,128)(2,1)}), bf16[6400,1600]{1,0:T(8,128)(2,1)}) %all-gather.23.cloned.1.call-update) | async-done | bytes 20480016 | tf_op jit(solution)/shard_map/all_gather | solution.py:49
  614.2 11.8 fusion.108
  626.0 12.7 multiply_reduce_fusion
  646.3 598.5 %while.31 = (s32[]{:T(128)}, f32[128,25,64]{0,2,1:T(8,128)}, f32[4,512,25,64]{1,0,3,2:T(4,128)}, f32[4,512,25,64]{1,0,3,2:T(4,128)}, bf16[4,512,25,64]{1,3,2,0:T...) while((s32[]{:T(128)}, f32[128,25,64]{0,2,1:T(8,128)}, ...), condition=%wide.region_12.13_spmd.clone, body=%wide.region_11.12_spmd.clone.sunk | while | flops 1067073536 | bytes 77246696 | solution.py:191
  669.9 63.3 %dynamic_update_slice.11 = f32[4,512,25,64]{1,0,3,2:T(4,128)} dynamic-update-slice(f32[4,512,25,64]{1,0,3,2:T(4,128)} %get-tuple-element.552, f32[1,512,25,64]{1,0,3,2:T(1,128)} %copy.106, s32[]{:T(128)S(6)} %copy.132, s32[]{:T(128)} %constant.28.clone.1..sunk.1, s32[]{:T(128)} %constant.28.clone.1..sunk.1, s32[]{:T(128)} %constant.28.clone.1..sunk.1) | dynamic-update-slice | bytes 6553604 | tf_op jit(solution)/shard_map/while/body/jit(dynamic_update_index_in_dim)/dynamic_update_slice | solution.py:191
  733.2 63.0 %dynamic_update_slice.12 = f32[4,512,25,64]{1,0,3,2:T(4,128)} dynamic-update-slice(f32[4,512,25,64]{1,0,3,2:T(4,128)} %get-tuple-element.553, f32[1,512,25,64]{1,0,3,2:T(1,128)S(1)} %copy.107, s32[]{:T(128)S(6)} %copy.132, s32[]{:T(128)} %constant.28.clone.1..sunk.1, s32[]{:T(128)} %constant.28.clone.1..sunk.1, s32[]{:T(128)} %constant.28.clone.1..sunk.1) | dynamic-update-slice | bytes 6553604 | tf_op jit(solution)/shard_map/while/body/jit(dynamic_update_index_in_dim)/dynamic_update_slice | solution.py:191
  819.4 63.3 %dynamic_update_slice.11 = f32[4,512,25,64]{1,0,3,2:T(4,128)} dynamic-update-slice(f32[4,512,25,64]{1,0,3,2:T(4,128)} %get-tuple-element.552, f32[1,512,25,64]{1,0,3,2:T(1,128)} %copy.106, s32[]{:T(128)S(6)} %copy.132, s32[]{:T(128)} %constant.28.clone.1..sunk.1, s32[]{:T(128)} %constant.28.clone.1..sunk.1, s32[]{:T(128)} %constant.28.clone.1..sunk.1) | dynamic-update-slice | bytes 6553604 | tf_op jit(solution)/shard_map/while/body/jit(dynamic_update_index_in_dim)/dynamic_update_slice | solution.py:191
  882.7 63.0 %dynamic_update_slice.12 = f32[4,512,25,64]{1,0,3,2:T(4,128)} dynamic-update-slice(f32[4,512,25,64]{1,0,3,2:T(4,128)} %get-tuple-element.553, f32[1,512,25,64]{1,0,3,2:T(1,128)S(1)} %copy.107, s32[]{:T(128)S(6)} %copy.132, s32[]{:T(128)} %constant.28.clone.1..sunk.1, s32[]{:T(128)} %constant.28.clone.1..sunk.1, s32[]{:T(128)} %constant.28.clone.1..sunk.1) | dynamic-update-slice | bytes 6553604 | tf_op jit(solution)/shard_map/while/body/jit(dynamic_update_index_in_dim)/dynamic_update_slice | solution.py:191
  968.9 63.3 %dynamic_update_slice.11 = f32[4,512,25,64]{1,0,3,2:T(4,128)} dynamic-update-slice(f32[4,512,25,64]{1,0,3,2:T(4,128)} %get-tuple-element.552, f32[1,512,25,64]{1,0,3,2:T(1,128)} %copy.106, s32[]{:T(128)S(6)} %copy.132, s32[]{:T(128)} %constant.28.clone.1..sunk.1, s32[]{:T(128)} %constant.28.clone.1..sunk.1, s32[]{:T(128)} %constant.28.clone.1..sunk.1) | dynamic-update-slice | bytes 6553604 | tf_op jit(solution)/shard_map/while/body/jit(dynamic_update_index_in_dim)/dynamic_update_slice | solution.py:191
  1032.1 63.0 %dynamic_update_slice.12 = f32[4,512,25,64]{1,0,3,2:T(4,128)} dynamic-update-slice(f32[4,512,25,64]{1,0,3,2:T(4,128)} %get-tuple-element.553, f32[1,512,25,64]{1,0,3,2:T(1,128)S(1)} %copy.107, s32[]{:T(128)S(6)} %copy.132, s32[]{:T(128)} %constant.28.clone.1..sunk.1, s32[]{:T(128)} %constant.28.clone.1..sunk.1, s32[]{:T(128)} %constant.28.clone.1..sunk.1) | dynamic-update-slice | bytes 6553604 | tf_op jit(solution)/shard_map/while/body/jit(dynamic_update_index_in_dim)/dynamic_update_slice | solution.py:191
  1118.3 63.3 %dynamic_update_slice.11 = f32[4,512,25,64]{1,0,3,2:T(4,128)} dynamic-update-slice(f32[4,512,25,64]{1,0,3,2:T(4,128)} %get-tuple-element.552, f32[1,512,25,64]{1,0,3,2:T(1,128)} %copy.106, s32[]{:T(128)S(6)} %copy.132, s32[]{:T(128)} %constant.28.clone.1..sunk.1, s32[]{:T(128)} %constant.28.clone.1..sunk.1, s32[]{:T(128)} %constant.28.clone.1..sunk.1) | dynamic-update-slice | bytes 6553604 | tf_op jit(solution)/shard_map/while/body/jit(dynamic_update_index_in_dim)/dynamic_update_slice | solution.py:191
  1181.6 63.0 %dynamic_update_slice.12 = f32[4,512,25,64]{1,0,3,2:T(4,128)} dynamic-update-slice(f32[4,512,25,64]{1,0,3,2:T(4,128)} %get-tuple-element.553, f32[1,512,25,64]{1,0,3,2:T(1,128)S(1)} %copy.107, s32[]{:T(128)S(6)} %copy.132, s32[]{:T(128)} %constant.28.clone.1..sunk.1, s32[]{:T(128)} %constant.28.clone.1..sunk.1, s32[]{:T(128)} %constant.28.clone.1..sunk.1) | dynamic-update-slice | bytes 6553604 | tf_op jit(solution)/shard_map/while/body/jit(dynamic_update_index_in_dim)/dynamic_update_slice | solution.py:191
  1244.8 15.9 copy.103
  1260.7 16.2 copy.102
  1276.9 19.0 pad_maximum_fusion
  1297.6 26.2 convolution_multiply_fusion
  1323.8 507.8 %fusion.2 = f32[104,6400]{1,0:T(8,128)S(1)} fusion(f32[1600,6400]{1,0:T(8,128)} %convolution_multiply_fusion), kind=kCustom, calls=%all-reduce-scatter.2 | all-reduce-scatter fusion | flops 10649601 | bytes 43622912
  1832.6 29.2 %collective-permute-start.3 = (bf16[60,6400]{1,0:T(8,128)(2,1)}, bf16[60,6400]{1,0:T(8,128)(2,1)}, u32[]{:S(2)}, u32[]{:S(2)}) collective-permute-start(bf16[60,6400]{1,0:T(8,128)(2,1)} %slice.35), channel_id=1, source_target_pairs={{0,1},{1,2},{2,3},{3,4},{4,5},{5,6},{6,7},{7,8},{8,9},{9,10},{10,1... | collective-permute-start | bytes 2304008
  1863.3 12.3 concatenate.12
  1879.1 18.5 convolution_multiply_fusion.1
  1901.0 5.5 convolution_multiply_fusion.3
  1909.0 12.7 convolution_multiply_fusion.2
  1921.7 591.9 %fusion.103 = (f32[104,4800]{1,0:T(8,128)}, f32[112,1600]{1,0:T(8,128)S(1)}) fusion(f32[1600,4800]{1,0:T(8,128)} %convolution_multiply_fusion.2, f32[1600,1600]{1,0:T(8,128)} %convolution_multiply_fusion.3), kind=kCustom, calls=%all-reduce-scatter.3 | all-reduce-scatter fusion | flops 10854402 | bytes 43674112
  2514.4 28.0 %collective-permute-start.1 = (bf16[112,1600]{1,0:T(8,128)(2,1)}, bf16[112,1600]{1,0:T(8,128)(2,1)S(1)}, u32[]{:S(2)}, u32[]{:S(2)}) collective-permute-start(bf16[112,1600]{1,0:T(8,128)(2,1)} %convert.26), channel_id=1, source_target_pairs={{0,1},{1,2},{2,3},{3,4},{4,5},{5,6},{6,7},{7,8},{8,9},{9,10},{10,1... | collective-permute-start | bytes 1075208
  2554.4 7.2 concatenate.11
  2566.5 11.6 concatenate.10
  2581.2 9.3 fusion.82
  2590.6 9.6 all-reduce.20
  2608.5 14.7 fusion.67
  2624.2 59.8 %all-reduce.19 = (f32[800]{0:T(1024)}, f32[800]{0:T(1024)}, f32[800,2]{0,1:T(2,128)}, f32[800]{0:T(1024)}, f32[800]{0:T(1024)}, /*index=5*/f32[800]{0:T(1024)}, f32[3200]{0:T(1024)}, f32[800]{0:T(1024)}) all-reduce(f32[800]{0:T(1024)S(1)} %dynamic-slice_convert_fusion.9, ...), channel_id=1, replica_groups=mesh['fsdp'=2,'context'=16] {'context'}, use_global_device_ids=true, to_apply=%region_18.19 | all-reduce | flops 9600 | bytes 73600 | tf_op jit(solution)/shard_map/psum | solution.py:291
  (325 shorter events, 211.6 us)
Async XLA Ops:
  7.2 35.4 %all-gather.21.cloned.1.call-start = ((), (), s32[]{:S(2)}) async-start(), calls=%async_computation.9 | async-start | bytes 1996800 | tf_op jit(solution)/shard_map/all_gather | solution.py:55
  7.9 161.5 %all-gather.25.cloned.1.call-start = ((), (), s32[]{:S(2)}) async-start(), calls=%async_computation.13 | async-start | bytes 17199104 | tf_op jit(solution)/shard_map/all_gather | solution.py:48
  8.0 21.9 copy-start.24
  27.2 15.9 copy-start.36
  27.2 17.2 copy-start.37
  27.2 17.4 copy-start.38
  27.2 17.6 copy-start.39
  27.3 17.9 copy-start.40
  27.3 18.1 copy-start.41
  27.3 27.1 %copy-start.35 = (bf16[800,2]{0,1:T(2,128)(2,1)S(1)}, bf16[800,2]{0,1:T(2,128)(2,1)}, u32[]{:S(2)}) copy-start(bf16[800,2]{0,1:T(2,128)(2,1)} %param.25) | copy-start | bytes 9604
  29.1 29.8 %copy-start.5 = (bf16[1,128,1600]{1,2,0:T(8,128)(2,1)S(1)}, bf16[1,128,1600]{1,2,0:T(8,128)(2,1)}, u32[]{:S(2)}) copy-start(bf16[1,128,1600]{1,2,0:T(8,128)(2,1)} %param.19) | copy-start | bytes 1228804
  29.1 173.6 %all-gather.31.cloned.1.call-start = ((), (), s32[]{:S(2)}) async-start(), calls=%async_computation.16 | async-start | bytes 2150400 | tf_op jit(solution)/shard_map/all_gather | solution.py:56
  29.8 225.1 %all-gather.27.cloned.1.call-start = ((), (), s32[]{:S(2)}) async-start(), calls=%async_computation.14 | async-start | bytes 5883904 | tf_op jit(solution)/shard_map/all_gather | solution.py:49
  42.5 323.0 %all-gather.29.cloned.1.call-start = ((), (), s32[]{:S(2)}) async-start(), calls=%async_computation.15 | async-start | bytes 22630400 | tf_op jit(solution)/shard_map/all_gather | solution.py:48
  43.1 392.2 %all-gather.19.cloned.1.call-start = ((), (), s32[]{:S(2)}) async-start(), calls=%async_computation.8 | async-start | bytes 6963200 | tf_op jit(solution)/shard_map/all_gather | solution.py:240
  54.3 131.2 %copy-start.20 = (f32[1600]{0:T(1024)}, f32[1600]{0:T(1024)S(1)}, u32[]{:S(2)}) copy-start(f32[1600]{0:T(1024)S(1)} %convert_element_type.185) | copy-start | bytes 19204
  58.8 126.7 %copy-start.18 = (f32[1600]{0:T(1024)}, f32[1600]{0:T(1024)S(1)}, u32[]{:S(2)}) copy-start(f32[1600]{0:T(1024)S(1)} %convert_element_type.184) | copy-start | bytes 19204
  59.1 126.4 %copy-start.30 = (f32[128]{0:T(128)}, f32[128]{0:T(128)S(1)}, u32[]{:S(2)}) copy-start(f32[128]{0:T(128)S(1)} %broadcast_multiply_fusion.5) | copy-start | bytes 1540
  59.3 126.2 %copy-start.32 = (f32[128]{0:T(128)}, f32[128]{0:T(128)S(1)}, u32[]{:S(2)}) copy-start(f32[128]{0:T(128)S(1)} %add_rsqrt_fusion.1) | copy-start | bytes 1540
  200.6 302.8 %all-gather.17.cloned.1.call-start = ((), (), s32[]{:S(2)}) async-start(), calls=%async_computation.7 | async-start | bytes 6963200 | tf_op jit(solution)/shard_map/all_gather | solution.py:239
  202.6 4.5 copy-start.44
  202.6 4.7 copy-start.34
  202.6 411.6 %all-gather.23.cloned.1.call-start = ((), (), s32[]{:S(2)}) async-start(), calls=%async_computation.10 | async-start | bytes 22630400 | tf_op jit(solution)/shard_map/all_gather | solution.py:49
  207.0 1699.5 %reduce-scatter.24.cloned.1.call-start = ((), (), s32[]{:S(2)}) async-start(), calls=%async_computation.11 | async-start | bytes 27852800 | tf_op jit(solution)/shard_map/reduce_scatter | solution.py:197
  207.3 354.8 %copy-start.22 = (f32[1600]{0:T(1024)}, f32[1600]{0:T(1024)S(1)}, u32[]{:S(2)}) copy-start(f32[1600]{0:T(1024)S(1)} %convert_element_type.198) | copy-start | bytes 19204
  556.8 5.0 copy-start.11
  561.8 76.9 %copy-start = (f32[128,1600]{0,1:T(8,128)}, f32[128,1600]{0,1:T(8,128)S(1)}, u32[]{:S(2)}) copy-start(f32[128,1600]{0,1:T(8,128)S(1)} %get-tuple-element.356) | copy-start | bytes 2457604
  562.1 52.1 %copy-start.14 = (bf16[1,128,1600]{1,2,0:T(8,128)(2,1)S(1)}, bf16[1,128,1600]{1,2,0:T(8,128)(2,1)}, u32[]{:S(2)}) copy-start(bf16[1,128,1600]{1,2,0:T(8,128)(2,1)} %param.20) | copy-start | bytes 1228804
  626.0 12.7 copy-start.9
  640.0 5.1 copy-start.7
  1295.9 1267.8 %reduce-scatter.34.cloned.1.call-start = ((), (), s32[]{:S(2)}) async-start(), calls=%async_computation.20 | async-start | bytes 2457600
  1323.8 538.1 %copy-start.43 = (u32[32]{0:T(128)S(1)}, u32[32]{0:T(128)}, u32[]{:S(2)}) copy-start(u32[32]{0:T(128)} %constant.134) | copy-start | bytes 388
  1832.6 30.6 %collective-permute-start.3 = (bf16[60,6400]{1,0:T(8,128)(2,1)}, bf16[60,6400]{1,0:T(8,128)(2,1)}, u32[]{:S(2)}, u32[]{:S(2)}) collective-permute-start(bf16[60,6400]{1,0:T(8,128)(2,1)} %slice.35), channel_id=1, source_target_pairs={{0,1},{1,2},{2,3},{3,4},{4,5},{5,6},{6,7},{7,8},{8,9},{9,10},{10,1... | collective-permute-start | bytes 2304008
  1879.0 721.6 %reduce-scatter.26.cloned.1.call-start = ((), (), s32[]{:S(2)}) async-start(), calls=%async_computation.12 | async-start | bytes 45260800 | tf_op jit(solution)/shard_map/reduce_scatter | solution.py:73
  1897.7 725.5 %reduce-scatter.30.cloned.1.call-start = ((), (), s32[]{:S(2)}) async-start(), calls=%async_computation.18 | async-start | bytes 614400
  1900.8 7.2 copy-start.16
  1901.0 7.9 copy-start.6
  1901.0 7.9 copy-start.19
  1901.0 7.9 copy-start.21
  1901.0 7.9 copy-start.31
  1901.0 7.9 copy-start.33
  2514.4 40.0 %collective-permute-start.1 = (bf16[112,1600]{1,0:T(8,128)(2,1)}, bf16[112,1600]{1,0:T(8,128)(2,1)S(1)}, u32[]{:S(2)}, u32[]{:S(2)}) collective-permute-start(bf16[112,1600]{1,0:T(8,128)(2,1)} %convert.26), channel_id=1, source_target_pairs={{0,1},{1,2},{2,3},{3,4},{4,5},{5,6},{6,7},{7,8},{8,9},{9,10},{10,1... | collective-permute-start | bytes 1075208
  2543.8 19.9 copy-start.25
  2543.9 10.5 collective-permute-start.2
  2551.0 15.4 collective-permute-start
  2554.3 129.7 %reduce-scatter.32.cloned.1.call-start = ((), (), s32[]{:S(2)}) async-start(), calls=%async_computation.19 | async-start | bytes 614400
  2563.7 122.2 %reduce-scatter.28.cloned.1.call-start = ((), (), s32[]{:S(2)}) async-start(), calls=%async_computation.17 | async-start | bytes 1843200
  2581.1 107.2 %reduce-scatter.36.cloned.1.call-start = ((), (), s32[]{:S(2)}) async-start(), calls=%async_computation.21 | async-start | bytes 2457600
  (22 other events, 60.9 us)
Sparse Core Ops, SparseCore 0:
  9.6 32.3 all-gather.20
  44.8 124.5 all-gather.24
  170.9 23.8 all-gather.30
  197.4 57.5 all-gather.26
  256.4 108.9 all-gather.28
  368.0 67.2 all-gather.18
  438.0 65.3 all-gather.16
  505.6 108.5 all-gather.22
  1296.0 427.5 reduce-scatter.23
  1879.2 37.8 reduce-scatter.33
  1921.9 617.4 reduce-scatter.25
  2554.4 11.3 reduce-scatter.29
  2568.7 13.3 reduce-scatter.31
  2584.2 23.3 reduce-scatter.27
  2609.7 26.7 reduce-scatter.35
where the time goes:
time: 2720 us; the launch traced here: 2700 us
  blocking collectives  1220 us (45%)
  local copies, waits for them, and re-layouts  727 us (27%)
  waiting for transfers between devices  396 us (15%)
  matrix products  229 us (8%)
  starting transfers between devices  65 us (2%)
  other arithmetic  44.6 us (2%)
    unnamed x4, blocking collectives  1120 us
    dynamic_update_slice x16, local copies, waits for them, and re-layouts, attend_backward(): lax.scan(step_whole, start_grad, (key_blocks, value_blocks, pos_blocks))  539 us
    all_gather x2, waiting for transfers between devices, gather_rows(): lax.all_gather(first, 'context', axis=0, tiled=True)  212 us
    unnamed x128, local copies, waits for them, and re-layouts  148 us
    all_gather x2, waiting for transfers between devices, gather_rows(): lax.all_gather(second, 'context', axis=0, tiled=True)  81.9 us
    unnamed x9, starting transfers between devices  64.6 us
    psum x1, blocking collectives, body(): lax.psum((attn_grads[2], attn_grads[3], attn_grads[4], attn_grads[5], mlp...  59.8 us
  transfers between devices with their start and end apart: 19, of which 7 were waited for; matrix products, arithmetic and copies ran while one was open for 52% of the time, Pallas kernels for 0%

commit v1 on v0

--- a/solution.py
+++ b/solution.py
@@ -12,6 +12,25 @@
 NEG_LARGE = -1e30
 
 
+def state_shifts_all(load):
+    e_now, y, b_next = (jax.lax.axis_size("context"), jax.lax.axis_index("context"), load.shape[0])
+    chunks = [(ix, (ix + 1) % e_now) for ix in range(e_now)]
+    so_far_all = [(ix, (ix - 1) % e_now) for ix in range(e_now)]
+    vec_out = jnp.zeros((*load.shape[:0], e_now * b_next, *load.shape[1:]), load.dtype)
+    vec_out = lax.dynamic_update_slice_in_dim(vec_out, load, y * b_next, axis=0)
+    v_next = arr_out = load
+    aux = e_now // 2
+    for q in range(1, aux + 1):
+        v_next = jax.lax.ppermute(v_next, "context", chunks)
+        vec_out = lax.dynamic_update_slice_in_dim(vec_out, v_next, (y - q) % e_now * b_next, axis=0)
+        if q < e_now - aux:
+            arr_out = jax.lax.ppermute(arr_out, "context", so_far_all)
+            vec_out = lax.dynamic_update_slice_in_dim(
+                vec_out, arr_out, (y + q) % e_now * b_next, axis=0
+            )
+    return vec_out
+
+
 def normalize(values, gain_vec, bias_vec):
     centred = values - jnp.mean(values, axis=-1, keepdims=True)
     inv_std = lax.rsqrt(jnp.mean(centred * centred, axis=-1, keepdims=True) + EPSILON)
@@ -44,10 +63,7 @@
 
 
 def gather_rows(first, second):
-    return (
-        lax.all_gather(first, "context", axis=0, tiled=True),
-        lax.all_gather(second, "context", axis=0, tiled=True),
-    )
+    return (lax.all_gather(first, "context", axis=0, tiled=True), state_shifts_all(second))
 
 
 def gather_cols(first, second, vec_a, vec_b, vec_c, vec_d):

time: 2720 us -> 2900 us (1.066)
  starting transfers between devices: 65 us -> 293 us
  waiting for transfers between devices: 396 us -> 257 us
  local copies, waits for them, and re-layouts: 727 us -> 798 us
    ppermute x0 -> x30, starting transfers between devices: none -> 222 us  [the longest x16 192 us: state_shifts_all(): v_next = jax.lax.ppermute(v_next, 'context', chunks)]
    ppermute x0 -> x30, waiting for transfers between devices: none -> 126 us  [the longest x16 96.9 us: state_shifts_all(): v_next = jax.lax.ppermute(v_next, 'context', chunks)]
    all_gather x2, waiting for transfers between devices: 212 us -> 116 us  [gather_rows(): lax.all_gather(first, 'context', axis=0, tiled=True)]
    all_gather x2 -> x0, waiting for transfers between devices: 81.9 us -> none  [gather_rows(): lax.all_gather(second, 'context', axis=0, tiled=True)]
    dynamic_update_slice x0 -> x32, local copies, waits for them, and re-layouts: none -> 77.2 us  [the longest x16 38 us: state_shifts_all(): lax.dynamic_update_slice_in_dim(vec_out, v_next, (y - q) % e_now * b_next...]
    all_gather x1, waiting for transfers between devices: 52.6 us -> 0.01 us  [body(): lax.all_gather(value_rows, 'context', axis=0, tiled=True)]
    all_gather x1, waiting for transfers between devices: 46.5 us -> 0.01 us  [body(): lax.all_gather(key_rows, 'context', axis=0, tiled=True)]
    unnamed x128 -> x161, local copies, waits for them, and re-layouts: 148 us -> 139 us
  transfers between devices with their start and end apart: 19 -> 47, of which waited for: 7 -> 14; matrix products, arithmetic and copies ran while one was open for 52% -> 49% of each run, Pallas kernels for 0% -> 0%
where the time goes in v1:
time: 2900 us; the launch traced here: 2870 us
  blocking collectives  1200 us (41%)
  local copies, waits for them, and re-layouts  798 us (28%)
  starting transfers between devices  293 us (10%)
  waiting for transfers between devices  257 us (9%)
  matrix products  248 us (9%)
  other arithmetic  54.3 us (2%)
    unnamed x4, blocking collectives  1100 us
    dynamic_update_slice x16, local copies, waits for them, and re-layouts, attend_backward(): lax.scan(step_whole, start_grad, (key_blocks, value_blocks, pos_blocks))  532 us
    ppermute x16, starting transfers between devices, state_shifts_all(): v_next = jax.lax.ppermute(v_next, 'context', chunks)  192 us
    unnamed x161, local copies, waits for them, and re-layouts  139 us
    all_gather x2, waiting for transfers between devices, gather_rows(): lax.all_gather(first, 'context', axis=0, tiled=True)  116 us
    ppermute x16, waiting for transfers between devices, state_shifts_all(): v_next = jax.lax.ppermute(v_next, 'context', chunks)  96.9 us
    unnamed x9, starting transfers between devices  70.8 us
    psum x1, blocking collectives, body(): lax.psum((attn_grads[2], attn_grads[3], attn_grads[4], attn_grads[5], mlp...  61.2 us
  transfers between devices with their start and end apart: 47, of which 14 were waited for; matrix products, arithmetic and copies ran while one was open for 49% of the time, Pallas kernels for 0%

profile of v1, /device:TPU:0, one launch (start us, length us, event | category | flops | bytes accessed | tf_op | source)
XLA Modules:
  0.0 2871.0 jit_solution(3546585873264735909)
XLA Ops:
  8.0 18.2 all-gather
  49.5 115.8 %all-gather.20.cloned.1.call-done = bf16[16,100,4800]{2,1,0:T(8,128)(2,1)} async-done(((bf16[1,100,4800]{2,1,0:T(8,128)(2,1)}), bf16[16,100,4800]{2,1,0:T(8,128)(2,1)}) %all-gather.20.cloned.1.call-update) | async-done | bytes 15360016 | tf_op jit(solution)/shard_map/all_gather | solution.py:66
  165.3 16.1 reshape.225
  181.5 10.5 fusion.102
  206.9 44.0 %collective-permute-done.15 = bf16[400,1600]{1,0:T(8,128)(2,1)S(1)} collective-permute-done((bf16[400,1600]{1,0:T(8,128)(2,1)S(1)}, bf16[400,1600]{1,0:T(8,128)(2,1)S(1)}, u32[]{:S(2)}, u32[]{:S(2)}) %collective-permute-start.15) | collective-permute-done | bytes 1280032 | tf_op jit(solution)/shard_map/ppermute | solution.py:24
  251.0 13.6 collective-permute-start.17
  264.6 23.2 collective-permute-done.17
  287.8 46.3 %collective-permute-start.19 = (bf16[400,1600]{1,0:T(8,128)(2,1)S(1)}, bf16[400,1600]{1,0:T(8,128)(2,1)}, u32[]{:S(2)}, u32[]{:S(2)}) collective-permute-start(bf16[400,1600]{1,0:T(8,128)(2,1)S(1)} %collective-permute-done.17), channel_id=1, source_target_pairs={{0,1},{1,2},{2,3},{3,4},{4,5},{5,6},{6,7},{7,8},{8,9},{9,10},{10,1... | collective-permute-start | bytes 3840008 | tf_op jit(solution)/shard_map/ppermute | solution.py:24
  336.8 46.6 %collective-permute-start.21 = (bf16[400,1600]{1,0:T(8,128)(2,1)}, bf16[400,1600]{1,0:T(8,128)(2,1)}, u32[]{:S(2)}, u32[]{:S(2)}) collective-permute-start(bf16[400,1600]{1,0:T(8,128)(2,1)} %collective-permute-done.19), channel_id=1, source_target_pairs={{0,1},{1,2},{2,3},{3,4},{4,5},{5,6},{6,7},{7,8},{8,9},{9,10},{10,1... | collective-permute-start | bytes 3840008 | tf_op jit(solution)/shard_map/ppermute | solution.py:24
  410.8 9.1 collective-permute-start.4
  421.2 15.5 collective-permute-start.6
  445.9 18.4 collective-permute-done.7
  469.0 27.9 collective-permute-start.10
  593.8 10.1 collective-permute-done.26
  610.9 13.4 collective-permute-start.29
  633.7 19.3 collective-permute-done.29
  654.3 17.2 reshape.231
  671.5 14.4 reshape.194
  693.1 14.4 reshape.196
  714.8 55.1 %while.30 = (s32[]{:T(128)}, f32[25,128]{1,0:T(8,128)S(1)}, f32[25,128]{1,0:T(8,128)S(1)}, f32[25,128,64]{1,2,0:T(8,128)S(1)}, s32[128]{0:T(128)S(1)}, /*index=5...) while((s32[]{:T(128)}, f32[25,128]{1,0:T(8,128)S(1)}, ...), condition=%wide.region_5.6_spmd.clone, body=%wide.region_2.5_spmd.clone.sunk | while | flops 438148736 | bytes 51673768 | solution.py:156
  775.5 12.1 convolution_add_fusion
  787.6 14.3 fusion.109
  801.9 12.5 multiply_reduce_fusion
  818.1 604.4 %while.31 = (s32[]{:T(128)}, f32[128,25,64]{0,2,1:T(8,128)}, f32[4,512,25,64]{1,0,3,2:T(4,128)}, f32[4,512,25,64]{1,0,3,2:T(4,128)}, bf16[4,512,25,64]{1,3,2,0:T...) while((s32[]{:T(128)}, f32[128,25,64]{0,2,1:T(8,128)}, ...), condition=%wide.region_12.13_spmd.clone, body=%wide.region_11.12_spmd.clone.sunk | while | flops 1067073536 | bytes 98545896 | solution.py:207
  835.2 63.0 %dynamic_update_slice.155 = f32[4,512,25,64]{1,0,3,2:T(4,128)} dynamic-update-slice(f32[4,512,25,64]{1,0,3,2:T(4,128)} %get-tuple-element.552, f32[1,512,25,64]{1,0,3,2:T(1,128)S(1)} %copy.106, s32[]{:T(128)S(6)} %copy.164, s32[]{:T(128)} %constant.186.clone.1..sunk.1, s32[]{:T(128)} %constant.186.clone.1..sunk.1, s32[]{:T(128)} %constant.186.clone.1..sunk.1) | dynamic-update-slice | bytes 6553604 | tf_op jit(solution)/shard_map/while/body/jit(dynamic_update_index_in_dim)/dynamic_update_slice | solution.py:207
  906.0 63.0 %dynamic_update_slice.156 = f32[4,512,25,64]{1,0,3,2:T(4,128)} dynamic-update-slice(f32[4,512,25,64]{1,0,3,2:T(4,128)} %get-tuple-element.553, f32[1,512,25,64]{1,0,3,2:T(1,128)S(1)} %copy.107, s32[]{:T(128)S(6)} %copy.164, s32[]{:T(128)} %constant.186.clone.1..sunk.1, s32[]{:T(128)} %constant.186.clone.1..sunk.1, s32[]{:T(128)} %constant.186.clone.1..sunk.1) | dynamic-update-slice | bytes 6553604 | tf_op jit(solution)/shard_map/while/body/jit(dynamic_update_index_in_dim)/dynamic_update_slice | solution.py:207
  986.2 63.0 %dynamic_update_slice.155 = f32[4,512,25,64]{1,0,3,2:T(4,128)} dynamic-update-slice(f32[4,512,25,64]{1,0,3,2:T(4,128)} %get-tuple-element.552, f32[1,512,25,64]{1,0,3,2:T(1,128)S(1)} %copy.106, s32[]{:T(128)S(6)} %copy.164, s32[]{:T(128)} %constant.186.clone.1..sunk.1, s32[]{:T(128)} %constant.186.clone.1..sunk.1, s32[]{:T(128)} %constant.186.clone.1..sunk.1) | dynamic-update-slice | bytes 6553604 | tf_op jit(solution)/shard_map/while/body/jit(dynamic_update_index_in_dim)/dynamic_update_slice | solution.py:207
  1057.0 63.0 %dynamic_update_slice.156 = f32[4,512,25,64]{1,0,3,2:T(4,128)} dynamic-update-slice(f32[4,512,25,64]{1,0,3,2:T(4,128)} %get-tuple-element.553, f32[1,512,25,64]{1,0,3,2:T(1,128)S(1)} %copy.107, s32[]{:T(128)S(6)} %copy.164, s32[]{:T(128)} %constant.186.clone.1..sunk.1, s32[]{:T(128)} %constant.186.clone.1..sunk.1, s32[]{:T(128)} %constant.186.clone.1..sunk.1) | dynamic-update-slice | bytes 6553604 | tf_op jit(solution)/shard_map/while/body/jit(dynamic_update_index_in_dim)/dynamic_update_slice | solution.py:207
  1137.2 63.0 %dynamic_update_slice.155 = f32[4,512,25,64]{1,0,3,2:T(4,128)} dynamic-update-slice(f32[4,512,25,64]{1,0,3,2:T(4,128)} %get-tuple-element.552, f32[1,512,25,64]{1,0,3,2:T(1,128)S(1)} %copy.106, s32[]{:T(128)S(6)} %copy.164, s32[]{:T(128)} %constant.186.clone.1..sunk.1, s32[]{:T(128)} %constant.186.clone.1..sunk.1, s32[]{:T(128)} %constant.186.clone.1..sunk.1) | dynamic-update-slice | bytes 6553604 | tf_op jit(solution)/shard_map/while/body/jit(dynamic_update_index_in_dim)/dynamic_update_slice | solution.py:207
  1208.0 63.0 %dynamic_update_slice.156 = f32[4,512,25,64]{1,0,3,2:T(4,128)} dynamic-update-slice(f32[4,512,25,64]{1,0,3,2:T(4,128)} %get-tuple-element.553, f32[1,512,25,64]{1,0,3,2:T(1,128)S(1)} %copy.107, s32[]{:T(128)S(6)} %copy.164, s32[]{:T(128)} %constant.186.clone.1..sunk.1, s32[]{:T(128)} %constant.186.clone.1..sunk.1, s32[]{:T(128)} %constant.186.clone.1..sunk.1) | dynamic-update-slice | bytes 6553604 | tf_op jit(solution)/shard_map/while/body/jit(dynamic_update_index_in_dim)/dynamic_update_slice | solution.py:207
  1288.3 63.0 %dynamic_update_slice.155 = f32[4,512,25,64]{1,0,3,2:T(4,128)} dynamic-update-slice(f32[4,512,25,64]{1,0,3,2:T(4,128)} %get-tuple-element.552, f32[1,512,25,64]{1,0,3,2:T(1,128)S(1)} %copy.106, s32[]{:T(128)S(6)} %copy.164, s32[]{:T(128)} %constant.186.clone.1..sunk.1, s32[]{:T(128)} %constant.186.clone.1..sunk.1, s32[]{:T(128)} %constant.186.clone.1..sunk.1) | dynamic-update-slice | bytes 6553604 | tf_op jit(solution)/shard_map/while/body/jit(dynamic_update_index_in_dim)/dynamic_update_slice | solution.py:207
  1359.0 63.0 %dynamic_update_slice.156 = f32[4,512,25,64]{1,0,3,2:T(4,128)} dynamic-update-slice(f32[4,512,25,64]{1,0,3,2:T(4,128)} %get-tuple-element.553, f32[1,512,25,64]{1,0,3,2:T(1,128)S(1)} %copy.107, s32[]{:T(128)S(6)} %copy.164, s32[]{:T(128)} %constant.186.clone.1..sunk.1, s32[]{:T(128)} %constant.186.clone.1..sunk.1, s32[]{:T(128)} %constant.186.clone.1..sunk.1) | dynamic-update-slice | bytes 6553604 | tf_op jit(solution)/shard_map/while/body/jit(dynamic_update_index_in_dim)/dynamic_update_slice | solution.py:207
  1422.5 16.0 copy.103
  1438.5 16.2 copy.102
  1454.7 19.0 pad_maximum_fusion
  1475.3 25.5 convolution_multiply_fusion
  1500.8 498.1 %fusion.2 = f32[104,6400]{1,0:T(8,128)S(1)} fusion(f32[1600,6400]{1,0:T(8,128)} %convolution_multiply_fusion), kind=kCustom, calls=%all-reduce-scatter.2 | all-reduce-scatter fusion | flops 10649601 | bytes 43622912
  1999.9 28.4 collective-permute-start.33
  2029.7 12.2 concatenate.12
  2045.4 18.2 convolution_multiply_fusion.1
  2074.9 12.8 convolution_multiply_fusion.2
  2087.6 585.4 %fusion.104 = (f32[104,4800]{1,0:T(8,128)}, f32[112,1600]{1,0:T(8,128)S(1)}) fusion(f32[1600,4800]{1,0:T(8,128)} %convolution_multiply_fusion.2, f32[1600,1600]{1,0:T(8,128)} %convolution_multiply_fusion.3), kind=kCustom, calls=%all-reduce-scatter.3 | all-reduce-scatter fusion | flops 10854402 | bytes 43674112
  2673.8 35.0 %collective-permute-start.31 = (bf16[112,1600]{1,0:T(8,128)(2,1)}, bf16[112,1600]{1,0:T(8,128)(2,1)S(1)}, u32[]{:S(2)}, u32[]{:S(2)}) collective-permute-start(bf16[112,1600]{1,0:T(8,128)(2,1)} %convert.26), channel_id=1, source_target_pairs={{0,1},{1,2},{2,3},{3,4},{4,5},{5,6},{6,7},{7,8},{8,9},{9,10},{10,1... | collective-permute-start | bytes 1075208
  2737.4 11.7 concatenate.10
  2752.1 9.3 fusion.83
  2761.5 10.2 all-reduce.20
  2780.1 14.7 fusion.68
  2795.8 61.2 %all-reduce.19 = (f32[800]{0:T(1024)}, f32[800]{0:T(1024)}, f32[800,2]{0,1:T(2,128)}, f32[800]{0:T(1024)}, f32[800]{0:T(1024)}, /*index=5*/f32[800]{0:T(1024)}, f32[3200]{0:T(1024)}, f32[800]{0:T(1024)}) all-reduce(f32[800]{0:T(1024)S(1)} %dynamic-slice_convert_fusion.9, ...), channel_id=1, replica_groups=mesh['fsdp'=2,'context'=16] {'context'}, use_global_device_ids=true, to_apply=%region_18.19 | all-reduce | flops 9600 | bytes 73600 | tf_op jit(solution)/shard_map/psum | solution.py:307
  (455 shorter events, 439.5 us)
Async XLA Ops:
  7.3 30.7 %all-gather.18.cloned.1.call-start = ((), (), s32[]{:S(2)}) async-start(), calls=%async_computation.9 | async-start | bytes 1996800 | tf_op jit(solution)/shard_map/all_gather | solution.py:71
  8.0 157.3 %all-gather.20.cloned.1.call-start = ((), (), s32[]{:S(2)}) async-start(), calls=%async_computation.12 | async-start | bytes 17199104 | tf_op jit(solution)/shard_map/all_gather | solution.py:66
  28.8 170.0 %all-gather.24.cloned.1.call-start = ((), (), s32[]{:S(2)}) async-start(), calls=%async_computation.14 | async-start | bytes 2150400 | tf_op jit(solution)/shard_map/all_gather | solution.py:72
  29.6 624.7 %all-gather.22.cloned.1.call-start = ((), (), s32[]{:S(2)}) async-start(), calls=%async_computation.13 | async-start | bytes 22630400 | tf_op jit(solution)/shard_map/all_gather | solution.py:66
  38.0 633.5 %all-gather.14.cloned.1.call-start = ((), (), s32[]{:S(2)}) async-start(), calls=%async_computation.7 | async-start | bytes 6963200 | tf_op jit(solution)/shard_map/all_gather | solution.py:255
  192.8 500.3 %all-gather.16.cloned.1.call-start = ((), (), s32[]{:S(2)}) async-start(), calls=%async_computation.8 | async-start | bytes 6963200 | tf_op jit(solution)/shard_map/all_gather | solution.py:256
  198.8 1873.7 %reduce-scatter.24.cloned.1.call-start = ((), (), s32[]{:S(2)}) async-start(), calls=%async_computation.10 | async-start | bytes 27852800 | tf_op jit(solution)/shard_map/reduce_scatter | solution.py:213
  202.4 48.5 %collective-permute-start.15 = (bf16[400,1600]{1,0:T(8,128)(2,1)S(1)}, bf16[400,1600]{1,0:T(8,128)(2,1)S(1)}, u32[]{:S(2)}, u32[]{:S(2)}) collective-permute-start(bf16[400,1600]{1,0:T(8,128)(2,1)S(1)} %bitcast.264), channel_id=1, source_target_pairs={{0,1},{1,2},{2,3},{3,4},{4,5},{5,6},{6,7},{7,8},{8,9},{9,10},{10,1... | collective-permute-start | bytes 3840008 | tf_op jit(solution)/shard_map/ppermute | solution.py:24
  202.5 62.0 %collective-permute-start.16 = (bf16[400,1600]{1,0:T(8,128)(2,1)S(1)}, bf16[400,1600]{1,0:T(8,128)(2,1)S(1)}, u32[]{:S(2)}, u32[]{:S(2)}) collective-permute-start(bf16[400,1600]{1,0:T(8,128)(2,1)S(1)} %bitcast.265), channel_id=1, source_target_pairs={{0,15},{1,0},{2,1},{3,2},{4,3},{5,4},{6,5},{7,6},{8,7},{9,8},{10,9... | collective-permute-start | bytes 3840008 | tf_op jit(solution)/shard_map/ppermute | solution.py:27
  251.0 36.8 %collective-permute-start.17 = (bf16[400,1600]{1,0:T(8,128)(2,1)S(1)}, bf16[400,1600]{1,0:T(8,128)(2,1)S(1)}, u32[]{:S(2)}, u32[]{:S(2)}) collective-permute-start(bf16[400,1600]{1,0:T(8,128)(2,1)S(1)} %collective-permute-done.15), channel_id=1, source_target_pairs={{0,1},{1,2},{2,3},{3,4},{4,5},{5,6},{6,7},{7,8},{8,9},{9,10},{10,1... | collective-permute-start | bytes 3840008 | tf_op jit(solution)/shard_map/ppermute | solution.py:24
  264.5 69.5 %collective-permute-start.18 = (bf16[400,1600]{1,0:T(8,128)(2,1)S(1)}, bf16[400,1600]{1,0:T(8,128)(2,1)}, u32[]{:S(2)}, u32[]{:S(2)}) collective-permute-start(bf16[400,1600]{1,0:T(8,128)(2,1)S(1)} %collective-permute-done.16), channel_id=1, source_target_pairs={{0,15},{1,0},{2,1},{3,2},{4,3},{5,4},{6,5},{7,6},{8,7},{9,8},{10,9... | collective-permute-start | bytes 3840008 | tf_op jit(solution)/shard_map/ppermute | solution.py:27
  287.8 49.1 %collective-permute-start.19 = (bf16[400,1600]{1,0:T(8,128)(2,1)S(1)}, bf16[400,1600]{1,0:T(8,128)(2,1)}, u32[]{:S(2)}, u32[]{:S(2)}) collective-permute-start(bf16[400,1600]{1,0:T(8,128)(2,1)S(1)} %collective-permute-done.17), channel_id=1, source_target_pairs={{0,1},{1,2},{2,3},{3,4},{4,5},{5,6},{6,7},{7,8},{8,9},{9,10},{10,1... | collective-permute-start | bytes 3840008 | tf_op jit(solution)/shard_map/ppermute | solution.py:24
  334.0 102.6 %collective-permute-start.20 = (bf16[400,1600]{1,0:T(8,128)(2,1)}, bf16[400,1600]{1,0:T(8,128)(2,1)}, u32[]{:S(2)}, u32[]{:S(2)}) collective-permute-start(bf16[400,1600]{1,0:T(8,128)(2,1)} %collective-permute-done.18), channel_id=1, source_target_pairs={{0,15},{1,0},{2,1},{3,2},{4,3},{5,4},{6,5},{7,6},{8,7},{9,8},{10,9... | collective-permute-start | bytes 3840008 | tf_op jit(solution)/shard_map/ppermute | solution.py:27
  336.8 99.8 %collective-permute-start.21 = (bf16[400,1600]{1,0:T(8,128)(2,1)}, bf16[400,1600]{1,0:T(8,128)(2,1)}, u32[]{:S(2)}, u32[]{:S(2)}) collective-permute-start(bf16[400,1600]{1,0:T(8,128)(2,1)} %collective-permute-done.19), channel_id=1, source_target_pairs={{0,1},{1,2},{2,3},{3,4},{4,5},{5,6},{6,7},{7,8},{8,9},{9,10},{10,1... | collective-permute-start | bytes 3840008 | tf_op jit(solution)/shard_map/ppermute | solution.py:24
  391.1 9.6 collective-permute-start
  393.1 16.5 collective-permute-start.1
  400.7 10.1 collective-permute-start.2
  409.5 10.4 collective-permute-start.3
  410.8 10.4 collective-permute-start.4
  419.9 19.5 collective-permute-start.5
  421.2 20.0 collective-permute-start.6
  436.7 95.9 %collective-permute-start.22 = (bf16[400,1600]{1,0:T(8,128)(2,1)}, bf16[400,1600]{1,0:T(8,128)(2,1)}, u32[]{:S(2)}, u32[]{:S(2)}) collective-permute-start(bf16[400,1600]{1,0:T(8,128)(2,1)} %collective-permute-done.20), channel_id=1, source_target_pairs={{0,15},{1,0},{2,1},{3,2},{4,3},{5,4},{6,5},{7,6},{8,7},{9,8},{10,9... | collective-permute-start | bytes 3840008 | tf_op jit(solution)/shard_map/ppermute | solution.py:27
  436.7 100.3 %collective-permute-start.23 = (bf16[400,1600]{1,0:T(8,128)(2,1)}, bf16[400,1600]{1,0:T(8,128)(2,1)}, u32[]{:S(2)}, u32[]{:S(2)}) collective-permute-start(bf16[400,1600]{1,0:T(8,128)(2,1)} %collective-permute-done.21), channel_id=1, source_target_pairs={{0,1},{1,2},{2,3},{3,4},{4,5},{5,6},{6,7},{7,8},{8,9},{9,10},{10,1... | collective-permute-start | bytes 3840008 | tf_op jit(solution)/shard_map/ppermute | solution.py:24
  439.4 24.8 collective-permute-start.7
  441.2 27.8 collective-permute-start.8
  464.2 40.5 %collective-permute-start.9 = (bf16[100,1600]{1,0:T(8,128)(2,1)}, bf16[100,1600]{1,0:T(8,128)(2,1)}, u32[]{:S(2)}, u32[]{:S(2)}) collective-permute-start(bf16[100,1600]{1,0:T(8,128)(2,1)} %collective-permute-done.7), channel_id=1, source_target_pairs={{0,15},{1,0},{2,1},{3,2},{4,3},{5,4},{6,5},{7,6},{8,7},{9,8},{10,9... | collective-permute-start | bytes 960008 | tf_op jit(solution)/shard_map/ppermute | solution.py:27
  469.0 35.8 %collective-permute-start.10 = (bf16[100,1600]{1,0:T(8,128)(2,1)}, bf16[100,1600]{1,0:T(8,128)(2,1)}, u32[]{:S(2)}, u32[]{:S(2)}) collective-permute-start(bf16[100,1600]{1,0:T(8,128)(2,1)} %collective-permute-done.8), channel_id=1, source_target_pairs={{0,1},{1,2},{2,3},{3,4},{4,5},{5,6},{6,7},{7,8},{8,9},{9,10},{10,1... | collective-permute-start | bytes 960008 | tf_op jit(solution)/shard_map/ppermute | solution.py:24
  504.8 24.4 collective-permute-start.11
  504.8 27.7 collective-permute-start.12
  529.2 36.6 %collective-permute-start.13 = (bf16[100,1600]{1,0:T(8,128)(2,1)}, bf16[100,1600]{1,0:T(8,128)(2,1)}, u32[]{:S(2)}, u32[]{:S(2)}) collective-permute-start(bf16[100,1600]{1,0:T(8,128)(2,1)} %collective-permute-done.11), channel_id=1, source_target_pairs={{0,15},{1,0},{2,1},{3,2},{4,3},{5,4},{6,5},{7,6},{8,7},{9,8},{10,9... | collective-permute-start | bytes 960008 | tf_op jit(solution)/shard_map/ppermute | solution.py:27
  532.5 36.2 %collective-permute-start.14 = (bf16[100,1600]{1,0:T(8,128)(2,1)}, bf16[100,1600]{1,0:T(8,128)(2,1)}, u32[]{:S(2)}, u32[]{:S(2)}) collective-permute-start(bf16[100,1600]{1,0:T(8,128)(2,1)} %collective-permute-done.12), channel_id=1, source_target_pairs={{0,1},{1,2},{2,3},{3,4},{4,5},{5,6},{6,7},{7,8},{8,9},{9,10},{10,1... | collective-permute-start | bytes 960008 | tf_op jit(solution)/shard_map/ppermute | solution.py:24
  532.5 44.0 %collective-permute-start.24 = (bf16[400,1600]{1,0:T(8,128)(2,1)}, bf16[400,1600]{1,0:T(8,128)(2,1)}, u32[]{:S(2)}, u32[]{:S(2)}) collective-permute-start(bf16[400,1600]{1,0:T(8,128)(2,1)} %collective-permute-done.22), channel_id=1, source_target_pairs={{0,15},{1,0},{2,1},{3,2},{4,3},{5,4},{6,5},{7,6},{8,7},{9,8},{10,9... | collective-permute-start | bytes 3840008 | tf_op jit(solution)/shard_map/ppermute | solution.py:27
  537.0 46.6 %collective-permute-start.25 = (bf16[400,1600]{1,0:T(8,128)(2,1)}, bf16[400,1600]{1,0:T(8,128)(2,1)}, u32[]{:S(2)}, u32[]{:S(2)}) collective-permute-start(bf16[400,1600]{1,0:T(8,128)(2,1)} %collective-permute-done.23), channel_id=1, source_target_pairs={{0,1},{1,2},{2,3},{3,4},{4,5},{5,6},{6,7},{7,8},{8,9},{9,10},{10,1... | collective-permute-start | bytes 3840008 | tf_op jit(solution)/shard_map/ppermute | solution.py:24
  576.6 27.3 collective-permute-start.26
  583.6 27.4 collective-permute-start.27
  603.9 28.7 %collective-permute-start.28 = (bf16[400,1600]{1,0:T(8,128)(2,1)S(1)}, bf16[400,1600]{1,0:T(8,128)(2,1)S(1)}, u32[]{:S(2)}, u32[]{:S(2)}) collective-permute-start(bf16[400,1600]{1,0:T(8,128)(2,1)S(1)} %collective-permute-done.26), channel_id=1, source_target_pairs={{0,15},{1,0},{2,1},{3,2},{4,3},{5,4},{6,5},{7,6},{8,7},{9,8},{10,9... | collective-permute-start | bytes 3840008 | tf_op jit(solution)/shard_map/ppermute | solution.py:27
  610.9 42.1 %collective-permute-start.29 = (bf16[400,1600]{1,0:T(8,128)(2,1)S(1)}, bf16[400,1600]{1,0:T(8,128)(2,1)S(1)}, u32[]{:S(2)}, u32[]{:S(2)}) collective-permute-start(bf16[400,1600]{1,0:T(8,128)(2,1)S(1)} %collective-permute-done.27), channel_id=1, source_target_pairs={{0,1},{1,2},{2,3},{3,4},{4,5},{5,6},{6,7},{7,8},{8,9},{9,10},{10,1... | collective-permute-start | bytes 3840008 | tf_op jit(solution)/shard_map/ppermute | solution.py:24
  1473.7 1261.0 %reduce-scatter.34.cloned.1.call-start = ((), (), s32[]{:S(2)}) async-start(), calls=%async_computation.18 | async-start | bytes 2457600
  1500.8 527.5 %copy-start.59 = (u32[32]{0:T(128)S(1)}, u32[32]{0:T(128)}, u32[]{:S(2)}) copy-start(u32[32]{0:T(128)} %constant.274) | copy-start | bytes 388
  1999.9 29.8 %collective-permute-start.33 = (bf16[60,6400]{1,0:T(8,128)(2,1)}, bf16[60,6400]{1,0:T(8,128)(2,1)}, u32[]{:S(2)}, u32[]{:S(2)}) collective-permute-start(bf16[60,6400]{1,0:T(8,128)(2,1)} %slice.35), channel_id=1, source_target_pairs={{0,1},{1,2},{2,3},{3,4},{4,5},{5,6},{6,7},{7,8},{8,9},{9,10},{10,1... | collective-permute-start | bytes 2304008
  2045.4 726.7 %reduce-scatter.26.cloned.1.call-start = ((), (), s32[]{:S(2)}) async-start(), calls=%async_computation.11 | async-start | bytes 45260800 | tf_op jit(solution)/shard_map/reduce_scatter | solution.py:89
  2063.7 731.0 %reduce-scatter.30.cloned.1.call-start = ((), (), s32[]{:S(2)}) async-start(), calls=%async_computation.16 | async-start | bytes 614400
  2673.8 51.5 %collective-permute-start.31 = (bf16[112,1600]{1,0:T(8,128)(2,1)}, bf16[112,1600]{1,0:T(8,128)(2,1)S(1)}, u32[]{:S(2)}, u32[]{:S(2)}) collective-permute-start(bf16[112,1600]{1,0:T(8,128)(2,1)} %convert.26), channel_id=1, source_target_pairs={{0,1},{1,2},{2,3},{3,4},{4,5},{5,6},{6,7},{7,8},{8,9},{9,10},{10,1... | collective-permute-start | bytes 1075208
  2712.5 24.9 collective-permute-start.30
  2717.7 7.5 collective-permute-start.32
  2720.8 136.3 %reduce-scatter.32.cloned.1.call-start = ((), (), s32[]{:S(2)}) async-start(), calls=%async_computation.17 | async-start | bytes 614400
  2734.6 124.3 %reduce-scatter.28.cloned.1.call-start = ((), (), s32[]{:S(2)}) async-start(), calls=%async_computation.15 | async-start | bytes 1843200
  2752.1 109.2 %reduce-scatter.36.cloned.1.call-start = ((), (), s32[]{:S(2)}) async-start(), calls=%async_computation.19 | async-start | bytes 2457600
  (71 other events, 2955.2 us)
Sparse Core Ops, SparseCore 0:
  9.6 28.2 all-gather.17
  40.7 124.5 all-gather.19
  166.9 23.8 all-gather.23
  192.2 215.2 all-gather.21
  410.0 101.8 all-gather.13
  514.5 114.1 all-gather.15
  1473.8 427.2 reduce-scatter.23
  2045.5 39.3 reduce-scatter.33
  2089.6 623.3 reduce-scatter.25
  2720.9 12.6 reduce-scatter.29
  2736.4 16.1 reduce-scatter.31
  2754.8 25.2 reduce-scatter.27
  2782.4 26.5 reduce-scatter.35
